TPU v7x, 32 devices: a whole 2x2x4 slice. The times are simulated.
32 devices in a mesh: seq: 8 (over y, x, core), wt: 4 (over z).
Axes of the slice: x: 2, y: 2, z: 4, core: 2. Of those that a mesh axis runs over, the one named last changes fastest.
Arguments:
- hidden: bfloat16 [4, 4096, 1024], P('wt', 'seq'), may hold values from -6 to 6
- doc_ids: int32 [4, 4096], P('wt'), may hold values from 0 to 15, never falling along the last dimension, each value on 1 to 1024 neighbouring positions
- norm_gain: float32 [1024], replicated, may hold values from 0.1 to 1.9
- in_weight: float32 [1024, 4384], P('wt'), may hold values from -0.1875 to 0.1875
- conv_weight: float32 [4, 2304], replicated, may hold values from -3 to 3
- conv_bias: float32 [2304], replicated, may hold values from -0.5 to 0.5
- step_bias: float32 [32], replicated, may hold values from -12 to -4
- decay_log: float32 [32], replicated, may hold values from 0 to 2.77
- skip_gain: float32 [32], replicated, may hold values from 0.5 to 1.5
- out_gain: float32 [2048], replicated, may hold values from 0.1 to 1.9
- out_weight: float32 [2048, 1024], P('wt'), may hold values from -0.125 to 0.125
- cotangent: bfloat16 [4, 4096, 1024], P('wt', 'seq'), may hold values from -6 to 6
Outputs:
- output: bfloat16 [4, 4096, 1024], P('wt', 'seq')
- input_grad: float32 [4, 4096, 1024], P('wt', 'seq')
- norm_gain_grad: float32 [1024], replicated
- in_weight_grad: float32 [1024, 4384], P('wt')
- conv_weight_grad: float32 [4, 2304], replicated
- conv_bias_grad: float32 [2304], replicated
- step_bias_grad: float32 [32], replicated
- decay_log_grad: float32 [32], replicated
- skip_gain_grad: float32 [32], replicated
- out_gain_grad: float32 [2048], replicated
- out_weight_grad: float32 [2048, 1024], P('wt')
Inputs may be any that keep to these rules, and one draw needn't show every extreme that they name: `doc_ids`: along each stream the document numbers never fall; every document 0 to 15 has 1 to 1024 positions, and some document has exactly 1024.
All inputs are finite; a program needn't handle non-finite values.
Results may differ from a plain program's by a relative error of at most 0.0038.
The roundings to bfloat16 on the way count: a program that leaves them out, or rounds other values in their place, can miss the bound.
Values may be sent and summed in bfloat16 or wider, within the bound.
No kernel may reach another device: no remote copies, remote signals or barrier semaphores. Data moves between devices by JAX's collectives and lax.ppermute only.
A program may use at most 320 MiB of HBM per device.

v0:
```python
import jax
import jax.numpy as jnp
from jax import lax
from jax.sharding import PartitionSpec as P

BLOCK = 256


EPS = 1e-05
HIGH = lax.Precision.HIGHEST


def conv_silu(values, weight, bias_row, segment):
    summed = bias_row[None, :] + weight[0][None, :] * values
    for offset in range(1, weight.shape[0]):
        before = jnp.pad(values[:-offset], ((offset, 0), (0, 0)))
        same_doc = jnp.pad(segment[offset:] == segment[:-offset], (offset, 0))
        summed = summed + weight[offset][None, :] * jnp.where(same_doc[:, None], before, 0.0)
    return jax.nn.silu(summed)


def ssd_block(carried, inputs, decay_rate, skip_gain):
    states, prev_doc = carried
    x_block, b_block, c_block, step_block, doc_block = inputs
    cumul = jnp.cumsum(step_block * decay_rate[None, :], axis=0)
    length = doc_block.shape[0]
    row_pos = lax.broadcasted_iota(jnp.int32, (length, length), 0)
    col_pos = lax.broadcasted_iota(jnp.int32, (length, length), 1)
    within = (col_pos <= row_pos) & (doc_block[:, None] == doc_block[None, :])
    cumul_t = cumul.T
    spread = cumul_t[:, :, None] - cumul_t[:, None, :]
    weights_in = jnp.where(within[None], jnp.exp(jnp.where(within[None], spread, 0.0)), 0.0)
    intersection = jnp.dot(c_block, b_block.T, precision=HIGH)
    scaled = step_block[:, :, None] * x_block
    local_out = jnp.einsum("hij,jhp->ihp", intersection[None] * weights_in, scaled, precision=HIGH)
    carry_in = jnp.where((doc_block == prev_doc)[:, None], jnp.exp(cumul), 0.0)
    from_state = jnp.einsum("in,hpn->ihp", c_block, states, precision=HIGH) * carry_in[:, :, None]
    result = local_out + from_state + skip_gain[None, :, None] * x_block
    last_doc = doc_block[-1]
    tail = jnp.where((doc_block == last_doc)[:, None], jnp.exp(cumul[-1][None, :] - cumul), 0.0)
    kept_part = jnp.where(prev_doc == last_doc, jnp.exp(cumul[-1]), 0.0)
    new_states = kept_part[:, None, None] * states + jnp.einsum(
        "jh,jhp,jn->hpn", tail, scaled, b_block, precision=HIGH
    )
    return ((new_states, last_doc), result)


def ssd(x_act, b_act, c_act, steps_dt, decay_rate, skip_gain, doc_ids, block_len):
    total_len = x_act.shape[0]
    head_count = steps_dt.shape[1]
    head_size = x_act.shape[1] // head_count
    block_count = total_len // block_len
    x_blocks = x_act.reshape(block_count, block_len, head_count, head_size)
    b_blocks = b_act.reshape(block_count, block_len, b_act.shape[1])
    c_blocks = c_act.reshape(block_count, block_len, c_act.shape[1])
    dt_blocks = steps_dt.reshape(block_count, block_len, head_count)
    doc_blocks = doc_ids.reshape(block_count, block_len)
    start_carry = (
        jnp.zeros((head_count, head_size, b_act.shape[1]), jnp.float32),
        jnp.array(-1, jnp.int32),
    )
    step_fn = jax.checkpoint(
        lambda carried, inputs: ssd_block(carried, inputs, decay_rate, skip_gain)
    )
    final_carry, outputs = lax.scan(
        step_fn, start_carry, (x_blocks, b_blocks, c_blocks, dt_blocks, doc_blocks)
    )
    return (outputs.reshape(total_len, head_count * head_size), final_carry[0])


def head_mix(
    x_raw,
    bc_raw,
    dt_raw,
    conv_x,
    conv_bc,
    bias_x,
    bias_bc,
    step_bias,
    decay_log,
    skip_gain,
    doc_ids,
    block_len,
):
    x_act = conv_silu(x_raw, conv_x, bias_x, doc_ids)
    bc_act = conv_silu(bc_raw, conv_bc, bias_bc, doc_ids)
    state_dim = bc_raw.shape[1] // 2
    steps_dt = jax.nn.softplus(dt_raw + step_bias[None, :])
    decay_rate = -jnp.exp(decay_log)
    return ssd(
        x_act,
        bc_act[:, :state_dim],
        bc_act[:, state_dim:],
        steps_dt,
        decay_rate,
        skip_gain,
        doc_ids,
        block_len,
    )[0]


def contract_rows(left_side, right_side):
    return lax.dot_general(
        left_side, right_side, (((0,), (0,)), ((), ())), preferred_element_type=jnp.float32
    )


def contract_cols(left_side, right_side):
    return lax.dot_general(
        left_side, right_side, (((1,), (1,)), ((), ())), preferred_element_type=jnp.float32
    )


def on_device(
    hidden,
    doc_ids,
    norm_gain,
    in_weight,
    conv_weight,
    conv_bias,
    step_bias,
    decay_log,
    skip_gain,
    out_gain,
    out_weight,
    cotangent,
):
    seq_count = lax.axis_size("seq")
    seq_index = lax.axis_index("seq")
    inner = out_gain.shape[0]
    state_dim = (conv_weight.shape[1] - inner) // 2
    head_total = step_bias.shape[0]
    tokens = hidden[0].astype(jnp.float32)
    docs_all = doc_ids[0]
    w_in, w_out = (
        lax.all_gather(in_weight.astype(jnp.bfloat16), "wt", axis=0, tiled=True),
        lax.all_gather(out_weight.astype(jnp.bfloat16), "wt", axis=0, tiled=True),
    )
    ratio = lax.rsqrt(jnp.mean(tokens * tokens, axis=-1, keepdims=True) + EPS)
    normed = (tokens * ratio * norm_gain[None, :]).astype(jnp.bfloat16)
    proj = jnp.dot(normed, w_in, preferred_element_type=jnp.float32).astype(jnp.bfloat16)
    gate = proj[:, :inner].astype(jnp.float32)
    x_send = proj[:, inner : 2 * inner]
    bc_send = proj[:, 2 * inner : 2 * inner + 2 * state_dim]
    dt_send = proj[:, 2 * inner + 2 * state_dim :]
    head_count = head_total // seq_count
    channels = inner // seq_count
    x_start = seq_index * channels
    head_start = seq_index * head_count
    x_heads, dt_heads = (
        lax.all_to_all(x_send, "seq", split_axis=1, concat_axis=0, tiled=True),
        lax.all_to_all(dt_send, "seq", split_axis=1, concat_axis=0, tiled=True),
    )
    bc_full = lax.all_gather(bc_send, "seq", axis=0, tiled=True)
    conv_x = lax.dynamic_slice_in_dim(conv_weight, x_start, channels, 1)
    bias_x = lax.dynamic_slice_in_dim(conv_bias, x_start, channels, 0)
    bias_heads = lax.dynamic_slice_in_dim(step_bias, head_start, head_count, 0)
    decay_heads = lax.dynamic_slice_in_dim(decay_log, head_start, head_count, 0)
    skip_heads = lax.dynamic_slice_in_dim(skip_gain, head_start, head_count, 0)

    def local_mix(
        x_raw, bc_raw, dt_raw, cx_part, cbc_part, bx_part, bbc_part, sb_part, dl_part, sg_part
    ):
        return head_mix(
            x_raw,
            bc_raw,
            dt_raw,
            cx_part,
            cbc_part,
            bx_part,
            bbc_part,
            sb_part,
            dl_part,
            sg_part,
            docs_all,
            BLOCK,
        )

    mixed, pullback = jax.vjp(
        local_mix,
        x_heads.astype(jnp.float32),
        bc_full.astype(jnp.float32),
        dt_heads.astype(jnp.float32),
        conv_x,
        conv_weight[:, inner:],
        bias_x,
        conv_bias[inner:],
        bias_heads,
        decay_heads,
        skip_heads,
    )
    mixed_tok = lax.all_to_all(
        mixed.astype(jnp.bfloat16), "seq", split_axis=0, concat_axis=1, tiled=True
    ).astype(jnp.float32)
    silu_gate = jax.nn.silu(gate)
    gated = mixed_tok * silu_gate
    gnorm = lax.rsqrt(jnp.mean(gated * gated, axis=-1, keepdims=True) + EPS)
    final = (gated * gnorm * out_gain[None, :]).astype(jnp.bfloat16)
    output = (tokens + jnp.dot(final, w_out, preferred_element_type=jnp.float32)).astype(
        jnp.bfloat16
    )
    grad_out = cotangent[0]
    grad_float = grad_out.astype(jnp.float32)
    out_weight_part = contract_rows(final, grad_out)
    grad_final = contract_cols(grad_out, w_out)
    out_gain_part = jnp.sum(grad_final * gated * gnorm, axis=0)
    scaled_grad = grad_final * out_gain[None, :]
    grad_gated = gnorm * scaled_grad - gated * gnorm * gnorm * gnorm * jnp.mean(
        scaled_grad * gated, axis=-1, keepdims=True
    )
    grad_mixed = (grad_gated * silu_gate).astype(jnp.bfloat16)
    sigma = jax.nn.sigmoid(gate)
    grad_gate = grad_gated * mixed_tok * sigma * (1.0 + gate * (1.0 - sigma))
    grad_heads = lax.all_to_all(grad_mixed, "seq", split_axis=1, concat_axis=0, tiled=True).astype(
        jnp.float32
    )
    grad_x, grad_bc, grad_dt, grad_cx, grad_cbc, grad_bx, grad_bbc, grad_sb, grad_dl, grad_sg = (
        pullback(grad_heads)
    )
    grad_x_tok, grad_dt_tok = (
        lax.all_to_all(grad_x.astype(jnp.bfloat16), "seq", split_axis=0, concat_axis=1, tiled=True),
        lax.all_to_all(
            grad_dt.astype(jnp.bfloat16), "seq", split_axis=0, concat_axis=1, tiled=True
        ),
    )
    grad_bc_tok = lax.psum_scatter(
        grad_bc.astype(jnp.bfloat16), "seq", scatter_dimension=0, tiled=True
    )
    conv_w_part = lax.dynamic_update_slice_in_dim(
        jnp.zeros(conv_weight.shape, jnp.float32), grad_cx, x_start, 1
    )
    conv_w_part = conv_w_part.at[:, inner:].add(grad_cbc)
    conv_b_part = lax.dynamic_update_slice_in_dim(
        jnp.zeros(conv_bias.shape, jnp.float32), grad_bx, x_start, 0
    )
    conv_b_part = conv_b_part.at[inner:].add(grad_bbc)
    step_part = lax.dynamic_update_slice_in_dim(
        jnp.zeros(step_bias.shape, jnp.float32), grad_sb, head_start, 0
    )
    decay_part = lax.dynamic_update_slice_in_dim(
        jnp.zeros(decay_log.shape, jnp.float32), grad_dl, head_start, 0
    )
    skip_part = lax.dynamic_update_slice_in_dim(
        jnp.zeros(skip_gain.shape, jnp.float32), grad_sg, head_start, 0
    )
    grad_proj = jnp.concatenate(
        [grad_gate.astype(jnp.bfloat16), grad_x_tok, grad_bc_tok, grad_dt_tok], axis=1
    )
    in_weight_part = contract_rows(normed, grad_proj)
    grad_normed = contract_cols(grad_proj, w_in)
    norm_gain_part = jnp.sum(grad_normed * tokens * ratio, axis=0)
    scaled_in = grad_normed * norm_gain[None, :]
    input_grad = (
        grad_float
        + ratio * scaled_in
        - tokens * ratio * ratio * ratio * jnp.mean(scaled_in * tokens, axis=-1, keepdims=True)
    )
    norm_total, out_gain_total, conv_w_total, conv_b_total, step_total, decay_total, skip_total = (
        lax.psum(
            (
                norm_gain_part,
                out_gain_part,
                conv_w_part,
                conv_b_part,
                step_part,
                decay_part,
                skip_part,
            ),
            ("seq", "wt"),
        )
    )
    in_rows, out_rows = (
        lax.psum_scatter(in_weight_part, "wt", scatter_dimension=0, tiled=True),
        lax.psum_scatter(out_weight_part, "wt", scatter_dimension=0, tiled=True),
    )
    in_grad, out_grad = lax.psum((in_rows, out_rows), "seq")
    return (
        output[None],
        input_grad[None],
        norm_total,
        in_grad,
        conv_w_total,
        conv_b_total,
        step_total,
        decay_total,
        skip_total,
        out_gain_total,
        out_grad,
    )


def solution(mesh):
    placed = (
        P("wt", "seq", None),
        P("wt", None),
        P(),
        P("wt", None),
        P(),
        P(),
        P(),
        P(),
        P(),
        P(),
        P("wt", None),
        P("wt", "seq", None),
    )
    return jax.shard_map(
        on_device,
        mesh=mesh,
        in_specs=placed,
        out_specs=(
            P("wt", "seq", None),
            P("wt", "seq", None),
            P(),
            P("wt", None),
            P(),
            P(),
            P(),
            P(),
            P(),
            P(),
            P("wt", None),
        ),
        check_vma=False,
    )
```

profile of v0, /device:TPU:0, one launch (start us, length us, event | category | flops | bytes accessed | tf_op | source)
XLA Modules:
  0.0 1974.9 jit_solution(3308826500575103710)
XLA Ops:
  11.6 161.3 %all-gather.4.cloned.1.call-done = bf16[1024,4384]{0,1:T(8,128)(2,1)} async-done(((bf16[256,4384]{0,1:T(8,128)(2,1)}), bf16[1024,4384]{0,1:T(8,128)(2,1)}) %all-gather.4.cloned.1.call-update) | async-done | bytes 8978448 | tf_op jit(solution)/shard_map/all_gather | solution.py:136
  172.8 8.9 convolution_convert_fusion
  207.4 23.2 %all-to-all-done.1 = bf16[512,8,256]{0,2,1:T(8,128)(2,1)S(1)} async-done(((bf16[512,8,256]{0,2,1:T(8,128)(2,1)}), bf16[512,8,256]{0,2,1:T(8,128)(2,1)S(1)}, u32[]{:S(2)}, u32[]{:S(2)}) %all-to-all-start.1) | async-done | bytes 2097184 | tf_op jit(solution)/shard_map/all_to_all | solution.py:151
  231.7 5.3 fusion.107
  238.8 4.4 copy.119
  248.7 5.6 fusion.106
  262.4 256.3 %while.50 = (s32[]{:T(128)}, f32[4,64,128]{2,1,0:T(8,128)S(1)}, s32[]{:T(128)}, bf16[16,256,4,64]{1,3,2,0:T(8,128)(2,1)}, f32[16,4,64,128]{3,2,1,0:T(8,128)}, /*...) while((s32[]{:T(128)}, f32[4,64,128]{2,1,0:T(8,128)S(1)}, ...), condition=%wide.region_4.5_spmd.clone, body=%wide.region_1.4_spmd.clone.sunk | while | flops 505319936 | bytes 3524341 | solution.py:65
  529.1 29.0 %all_to_all.84 = bf16[8,512,256]{1,2,0:T(8,128)(2,1)S(1)} all-to-all(bf16[8,512,256]{1,2,0:T(8,128)(2,1)S(1)} %copy.123), channel_id=1, replica_groups=mesh['seq'=8,'wt'=4] {'seq'}, dimensions={0} | all-to-all | bytes 4194304 | tf_op jit(solution)/shard_map/all_to_all | solution.py:192
  558.2 5.8 multiply_reduce_fusion.15
  564.1 7.4 multiply_reduce_fusion.5
  571.5 5.6 fusion.94
  584.9 23.3 %all-to-all-done.3 = bf16[512,8,256]{0,2,1:T(8,128)(2,1)} async-done(((bf16[512,8,256]{0,2,1:T(8,128)(2,1)}), bf16[512,8,256]{0,2,1:T(8,128)(2,1)}, u32[]{:S(2)}, u32[]{:S(2)}) %all-to-all-start.3) | async-done | bytes 2097184 | tf_op jit(solution)/shard_map/all_to_all | solution.py:214
  610.3 4.4 copy.125
  614.8 5.0 reshape.563
  626.0 673.0 %while.51 = (s32[]{:T(128)}, f32[4]{0:T(128)}, f32[4]{0:T(128)}, f32[4,64,128]{2,1,0:T(8,128)S(1)}, f32[16,256,4,64]{1,0,3,2:T(8,128)}, /*index=5*/f32[16,256,12...) while((s32[]{:T(128)}, f32[4]{0:T(128)}, f32[4]{0:T(128)}, ...), condition=%wide.region_21.22_spmd.clone, body=%wide.region_7.21_spmd.clone.sunk | while | flops 1213779456 | bytes 13377388 | solution.py:65
  647.7 5.0 reduce-window.74
  655.3 7.0 dynamic_update_slice.106
  689.7 5.0 reduce-window.74
  697.4 7.0 dynamic_update_slice.106
  731.8 5.0 reduce-window.74
  739.4 7.0 dynamic_update_slice.106
  773.8 5.0 reduce-window.74
  781.5 7.0 dynamic_update_slice.106
  815.9 5.0 reduce-window.74
  823.5 7.0 dynamic_update_slice.106
  857.9 5.0 reduce-window.74
  865.6 7.0 dynamic_update_slice.106
  900.0 5.0 reduce-window.74
  907.6 7.0 dynamic_update_slice.106
  942.0 5.0 reduce-window.74
  949.7 7.0 dynamic_update_slice.106
  984.1 5.0 reduce-window.74
  991.7 7.0 dynamic_update_slice.106
  1026.2 5.0 reduce-window.74
  1033.8 7.0 dynamic_update_slice.106
  1068.2 5.0 reduce-window.74
  1075.9 7.0 dynamic_update_slice.106
  1110.3 5.0 reduce-window.74
  1117.9 7.0 dynamic_update_slice.106
  1152.3 5.0 reduce-window.74
  1160.0 7.0 dynamic_update_slice.106
  1194.4 5.0 reduce-window.74
  1202.0 7.0 dynamic_update_slice.106
  1236.4 5.0 reduce-window.74
  1244.1 7.0 dynamic_update_slice.106
  1278.5 5.0 reduce-window.74
  1286.1 7.0 dynamic_update_slice.106
  1299.1 7.9 copy.192
  1312.8 18.7 fusion.147
  1335.9 5.6 fusion.103
  1341.5 5.7 fusion.104
  1347.2 6.7 add_convert_fusion
  1354.1 8.0 fusion.121
  1367.2 8.1 add_convert_fusion.1
  1376.9 4.4 all-to-all-start.4
  1381.3 29.3 %all-to-all-done.4 = bf16[8,512,256]{1,2,0:T(8,128)(2,1)} async-done(((bf16[8,512,256]{1,2,0:T(8,128)(2,1)}), bf16[8,512,256]{1,2,0:T(8,128)(2,1)}, u32[]{:S(2)}, u32[]{:S(2)}) %all-to-all-start.4) | async-done | bytes 2097184 | tf_op jit(solution)/shard_map/all_to_all | solution.py:221
  1410.7 13.3 fusion.125
  1424.1 121.7 %reduce-scatter.8.cloned.1.call-done = f32[512,1024]{1,0:T(8,128)} async-done(((f32[2048,1024]{1,0:T(8,128)}), f32[512,1024]{1,0:T(8,128)}) %reduce-scatter.8.cloned.1.call-update) | async-done | bytes 2097168 | tf_op jit(solution)/shard_map/reduce_scatter | solution.py:274
  1545.8 302.2 %reduce-scatter.6.cloned.1.call-done = f32[256,4384]{0,1:T(8,128)} async-done(((f32[1024,4384]{0,1:T(8,128)}), f32[256,4384]{0,1:T(8,128)}) %reduce-scatter.6.cloned.1.call-update) | async-done | bytes 4489232 | tf_op jit(solution)/shard_map/reduce_scatter | solution.py:273
  1848.1 6.9 fusion.120
  1856.3 12.2 fusion.119
  1868.5 43.4 %all-reduce.27 = (f32[1024]{0:T(1024)}, f32[4,2304]{1,0:T(4,128)}, f32[2304]{0:T(1024)}, f32[32]{0:T(128)}, f32[32]{0:T(128)}, /*index=5*/f32[32]{0:T(128)}, f32[2048]{0:T(1024)}) all-reduce(f32[1024]{0:T(1024)S(1)} %get-tuple-element.838, f32[4,2304]{1,0:T(4,128)S(1)} %fusion.141, ...), channel_id=1, replica_groups=mesh['seq'=8,'wt'=4] {'seq','wt'}, use_global_device_ids=true, to_apply=%region_25.26 | all-reduce | flops 14688 | bytes 117504 | tf_op jit(solution)/shard_map/psum | solution.py:259
  1915.6 46.1 %all-reduce.31.cloned.1.call-done = (f32[256,4384]{0,1:T(8,128)}, f32[512,1024]{1,0:T(8,128)}) async-done(((f32[256,4384]{0,1:T(8,128)}, f32[512,1024]{1,0:T(8,128)}), (f32[256,4384]{0,1:T(8,128)}, f32[512,1024]{1,0:T(8,128)})) %all-reduce.31.cloned.1.call-update) | async-done | bytes 6586384 | tf_op jit(solution)/shard_map/psum | solution.py:276
  1961.7 4.8 copy.314
  (1652 shorter events, 786.5 us)
Async XLA Ops:
  7.2 165.6 %copy-start.63 = (f32[1024]{0:T(1024)S(1)}, f32[1024]{0:T(1024)}, u32[]{:S(2)}) copy-start(f32[1024]{0:T(1024)} %param.22) | copy-start | bytes 12292
  7.2 165.6 %all-gather.4.cloned.1.call-start = ((), (), s32[]{:S(2)}) async-start(), calls=%async_computation.9 | async-start | bytes 11223040 | tf_op jit(solution)/shard_map/all_gather | solution.py:136
  11.2 232.0 %all-gather.6.cloned.1.call-start = ((), (), s32[]{:S(2)}) async-start(), calls=%async_computation.10 | async-start | bytes 2359296 | tf_op jit(solution)/shard_map/all_gather | solution.py:154
  11.6 170.2 %copy-start.58 = (f32[512]{0:T(512)}, f32[512]{0:T(512)S(1)}, u32[]{:S(2)}) copy-start(f32[512]{0:T(512)S(1)} %add_rsqrt_fusion.1) | copy-start | bytes 6148
  186.0 8.7 all-to-all-start
  194.7 35.9 %all-to-all-start.1 = ((bf16[512,8,256]{0,2,1:T(8,128)(2,1)}), bf16[512,8,256]{0,2,1:T(8,128)(2,1)S(1)}, u32[]{:S(2)}, u32[]{:S(2)}) async-start(bf16[512,8,256]{0,2,1:T(8,128)(2,1)} %bitcast.461), calls=%async_computation.1 | async-start | bytes 4194304 | tf_op jit(solution)/shard_map/all_to_all | solution.py:151
  198.4 365.6 %all-gather.8.cloned.1.call-start = ((), (), s32[]{:S(2)}) async-start(), calls=%async_computation.11 | async-start | bytes 5242880 | tf_op jit(solution)/shard_map/all_gather | solution.py:137
  203.5 43.0 %copy-start.25 = (pred[4096]{0:T(1024)(128)(4,1)}, pred[4096]{0:T(1024)(128)(4,1)S(1)}, u32[]{:S(2)}) copy-start(pred[4096]{0:T(1024)(128)(4,1)S(1)} %pad.137) | copy-start | bytes 12292
  203.7 42.8 %copy-start.27 = (pred[4096]{0:T(1024)(128)(4,1)}, pred[4096]{0:T(1024)(128)(4,1)S(1)}, u32[]{:S(2)}) copy-start(pred[4096]{0:T(1024)(128)(4,1)S(1)} %pad.135) | copy-start | bytes 12292
  203.9 42.6 %copy-start.29 = (pred[4096]{0:T(1024)(128)(4,1)}, pred[4096]{0:T(1024)(128)(4,1)S(1)}, u32[]{:S(2)}) copy-start(pred[4096]{0:T(1024)(128)(4,1)S(1)} %pad.133) | copy-start | bytes 12292
  204.0 27.6 %copy-start.61 = (f32[4]{0:T(128)}, f32[4]{0:T(128)S(1)}, u32[]{:S(2)}) copy-start(f32[4]{0:T(128)S(1)} %dynamic_slice.123) | copy-start | bytes 52
  205.9 25.8 %copy-start.42 = (f32[1,256]{1,0:T(1,128)}, f32[1,256]{1,0:T(1,128)S(1)}, u32[]{:S(2)}) copy-start(f32[1,256]{1,0:T(1,128)S(1)} %get-tuple-element.945) | copy-start | bytes 3076
  205.9 25.8 %copy-start.46 = (f32[1,256]{1,0:T(1,128)}, f32[1,256]{1,0:T(1,128)S(1)}, u32[]{:S(2)}) copy-start(f32[1,256]{1,0:T(1,128)S(1)} %get-tuple-element.947) | copy-start | bytes 3076
  205.9 25.8 %copy-start.50 = (f32[1,256]{1,0:T(1,128)}, f32[1,256]{1,0:T(1,128)S(1)}, u32[]{:S(2)}) copy-start(f32[1,256]{1,0:T(1,128)S(1)} %get-tuple-element.943) | copy-start | bytes 3076
  205.9 25.8 %copy-start.54 = (f32[1,256]{1,0:T(1,128)}, f32[1,256]{1,0:T(1,128)S(1)}, u32[]{:S(2)}) copy-start(f32[1,256]{1,0:T(1,128)S(1)} %get-tuple-element.944) | copy-start | bytes 3076
  205.9 40.6 %copy-start.44 = (f32[1,256]{1,0:T(1,128)}, f32[1,256]{1,0:T(1,128)S(1)}, u32[]{:S(2)}) copy-start(f32[1,256]{1,0:T(1,128)S(1)} %get-tuple-element.942) | copy-start | bytes 3076
  205.9 40.6 %copy-start.48 = (f32[1,256]{1,0:T(1,128)}, f32[1,256]{1,0:T(1,128)S(1)}, u32[]{:S(2)}) copy-start(f32[1,256]{1,0:T(1,128)S(1)} %get-tuple-element.948) | copy-start | bytes 3076
  205.9 40.6 %copy-start.52 = (f32[1,256]{1,0:T(1,128)}, f32[1,256]{1,0:T(1,128)S(1)}, u32[]{:S(2)}) copy-start(f32[1,256]{1,0:T(1,128)S(1)} %get-tuple-element.949) | copy-start | bytes 3076
  206.0 40.6 %copy-start.56 = (f32[1,256]{1,0:T(1,128)}, f32[1,256]{1,0:T(1,128)S(1)}, u32[]{:S(2)}) copy-start(f32[1,256]{1,0:T(1,128)S(1)} %get-tuple-element.946) | copy-start | bytes 3076
  577.1 31.0 %all-to-all-start.3 = ((bf16[512,8,256]{0,2,1:T(8,128)(2,1)}), bf16[512,8,256]{0,2,1:T(8,128)(2,1)}, u32[]{:S(2)}, u32[]{:S(2)}) async-start(bf16[512,8,256]{0,2,1:T(8,128)(2,1)} %bitcast.459), calls=%async_computation.3 | async-start | bytes 4194304 | tf_op jit(solution)/shard_map/all_to_all | solution.py:214
  581.5 829.2 %reduce-scatter.4.cloned.1.call-start = ((), (), s32[]{:S(2)}) async-start(), calls=%async_computation.12 | async-start | bytes 2359296 | tf_op jit(solution)/shard_map/reduce_scatter | solution.py:226
  631.0 16.3 copy-start.7
  639.0 14.2 copy-start.39
  673.1 16.3 copy-start.7
  681.0 14.2 copy-start.39
  715.1 16.3 copy-start.7
  723.1 14.2 copy-start.39
  757.2 16.3 copy-start.7
  765.1 14.2 copy-start.39
  799.2 16.3 copy-start.7
  807.2 14.2 copy-start.39
  841.3 16.3 copy-start.7
  849.2 14.2 copy-start.39
  883.3 16.3 copy-start.7
  891.3 14.2 copy-start.39
  925.4 16.3 copy-start.7
  933.3 14.2 copy-start.39
  967.4 16.3 copy-start.7
  975.4 14.2 copy-start.39
  1009.5 16.3 copy-start.7
  1017.5 14.2 copy-start.39
  1051.5 16.3 copy-start.7
  1059.5 14.2 copy-start.39
  1093.6 16.3 copy-start.7
  1101.6 14.2 copy-start.39
  1135.7 16.3 copy-start.7
  1143.6 14.2 copy-start.39
  1177.7 16.3 copy-start.7
  1185.7 14.2 copy-start.39
  1219.8 16.3 copy-start.7
  1227.7 14.2 copy-start.39
  1261.8 16.3 copy-start.7
  1269.8 14.2 copy-start.39
  1312.8 18.8 copy-start.38
  1312.8 18.8 copy-start.55
  1312.8 18.8 copy-start.57
  1354.0 191.8 %reduce-scatter.8.cloned.1.call-start = ((), (), s32[]{:S(2)}) async-start(), calls=%async_computation.14 | async-start | bytes 10485760 | tf_op jit(solution)/shard_map/reduce_scatter | solution.py:274
  1363.7 13.2 all-to-all-start.5
  1375.3 35.4 %copy-start.15 = (bf16[1,512,1024]{2,1,0:T(8,128)(2,1)S(1)}, bf16[1,512,1024]{2,1,0:T(8,128)(2,1)}, u32[]{:S(2)}) copy-start(bf16[1,512,1024]{2,1,0:T(8,128)(2,1)} %param.20) | copy-start | bytes 3145732
  1375.4 35.3 %copy-start.59 = (f32[512]{0:T(512)S(1)}, f32[512]{0:T(512)}, u32[]{:S(2)}) copy-start(f32[512]{0:T(512)} %copy-done.58) | copy-start | bytes 6148
  1375.4 35.3 %copy-start.64 = (f32[1024]{0:T(1024)S(1)}, f32[1024]{0:T(1024)}, u32[]{:S(2)}) copy-start(f32[1024]{0:T(1024)} %param.22) | copy-start | bytes 12292
  1376.9 33.8 %all-to-all-start.4 = ((bf16[8,512,256]{1,2,0:T(8,128)(2,1)}), bf16[8,512,256]{1,2,0:T(8,128)(2,1)}, u32[]{:S(2)}, u32[]{:S(2)}) async-start(bf16[8,512,256]{1,2,0:T(8,128)(2,1)} %bitcast.298), calls=%async_computation.4 | async-start | bytes 4194304 | tf_op jit(solution)/shard_map/all_to_all | solution.py:221
  1381.3 466.8 %reduce-scatter.6.cloned.1.call-start = ((), (), s32[]{:S(2)}) async-start(), calls=%async_computation.13 | async-start | bytes 22446080 | tf_op jit(solution)/shard_map/reduce_scatter | solution.py:273
  1424.1 537.6 %all-reduce.31.cloned.1.call-start = ((), (), s32[]{:S(2)}) async-start(), calls=%async_computation.15 | async-start | bytes 13172736 | tf_op jit(solution)/shard_map/psum | solution.py:276
  (108 other events, 515.2 us)
Sparse Core Ops, SparseCore 0:
  11.3 161.4 all-gather.3
  184.7 37.7 all-gather.5
  224.6 79.9 all-gather.7
  1354.1 40.9 reduce-scatter.3
  1397.4 148.3 reduce-scatter.7
  1548.1 299.8 reduce-scatter.5
  1851.9 109.7 all-reduce.30
where the time goes:
time: 1990 us; the launch traced here: 1970 us
  waiting for transfers between devices  709 us (36%)
  local copies, waits for them, and re-layouts  434 us (22%)
  matrix products  358 us (18%)
  other arithmetic  320 us (16%)
  blocking collectives  72.4 us (4%)
  loops' own time  46.6 us (2%)
  starting transfers between devices  20.3 us (1%)
    reduce_scatter x1, waiting for transfers between devices, on_device(): lax.psum_scatter(in_weight_part, 'wt', scatter_dimension=0, tiled=True)  302 us
    all_gather x1, waiting for transfers between devices, on_device(): lax.all_gather(in_weight.astype(jnp.bfloat16), 'wt', axis=0, tiled=True)  161 us
    dynamic_update_slice x48, local copies, waits for them, and re-layouts, ssd(): lax.scan(step_fn, start_carry, (x_blocks, b_blocks, c_blocks, dt_blocks,...  151 us
    another operation x130, other arithmetic  145 us
    reduce_scatter x1, waiting for transfers between devices, on_device(): lax.psum_scatter(out_weight_part, 'wt', scatter_dimension=0, tiled=True)  122 us
    dot_general x48, matrix products, ssd_block(): jnp.einsum('hij,jhp->ihp', intersection[None] * weights_in, scaled, preci...  117 us
    dynamic_slice x64, local copies, waits for them, and re-layouts, ssd(): lax.scan(step_fn, start_carry, (x_blocks, b_blocks, c_blocks, dt_blocks,...  71.7 us
    dot_general x48, matrix products, ssd_block(): jnp.einsum('jh,jhp,jn->hpn', tail, scaled, b_block, precision=HIGH)  64.6 us
  transfers between devices with their start and end apart: 12, of which 8 were waited for; matrix products, arithmetic and copies ran while one was open for 18% of the time, Pallas kernels for 0%

commit v1 on v0

v1 whole, which is shorter than its diff:
```python
import functools

import jax
import jax.numpy as jnp
from jax import lax
from jax.experimental import pallas as pl
from jax.experimental.pallas import tpu as pltpu
from jax.sharding import PartitionSpec as P

EPS = 1e-05
LOG2E = 1.4426950408889634
CHUNK = 128
HALO = 16
LANES = 256
HEAD = 64
TAPS = 4
FULL = lax.Precision.HIGHEST
F32 = jnp.float32
BF16 = jnp.bfloat16
SEQ = "seq"
WT = "wt"


def mm(a, b):
    return jnp.dot(a, b, preferred_element_type=F32)


def mm_cols(a, b):
    return lax.dot_general(a, b, (((1,), (1,)), ((), ())), preferred_element_type=F32)


def mm_rows(a, b):
    return lax.dot_general(a, b, (((0,), (0,)), ((), ())), preferred_element_type=F32)


def sigmoid(x):
    return 0.5 * jnp.tanh(0.5 * x) + 0.5


def split2(x):
    high = x.astype(BF16)
    return high, (x - high.astype(F32)).astype(BF16)


def mm_split(x, ones):
    high, low = split2(x)
    return mm(high, ones) + mm(low, ones)


def mm3(a, b, mult=mm):
    a_high, a_low = a if isinstance(a, tuple) else split2(a)
    b_high, b_low = b if isinstance(b, tuple) else split2(b)
    return mult(a_high, b_high) + mult(a_high, b_low) + mult(a_low, b_high)


def pack3(x):
    high = x.astype(BF16).astype(F32)
    rest = x - high
    mid = rest.astype(BF16).astype(F32)
    low = rest - mid
    return (high + pltpu.roll(mid, 32, 1) + pltpu.roll(low, 64, 1)).astype(BF16)


def softplus(x):
    small = jnp.exp(-jnp.abs(x))
    series = small * (1.0 - small * (0.5 - small * (1.0 / 3.0 - small * (0.25 - small * 0.2))))
    return jnp.maximum(x, 0.0) + jnp.where(small < 0.02, series, jnp.log(1.0 + small))


def conv_inputs(window, shifts):
    moved = mm(shifts, window)
    return [window[HALO:].astype(F32)] + [
        moved[j * CHUNK : (j + 1) * CHUNK] for j in range(TAPS - 1)
    ]


def conv_sum(taps, cw):
    total = cw[TAPS : TAPS + 1]
    for j in range(TAPS):
        total = total + cw[j : j + 1] * taps[j]
    return total


def pair_cols(x):
    return x[:, :128], x[:, 128:]


def pair_rows(x):
    return x[:128], x[128:]


def rows_of(c):
    return slice(c * CHUNK, (c + 1) * CHUNK)


def window_of(c):
    return slice(c * CHUNK, (c + 1) * CHUNK + HALO)


def prep_kernel(
    bc_ref, dtr_ref, sh_ref, mask_ref, cols_ref, cw_ref, hp_ref,
    b_ref, c_ref, bt_ref, ct_ref, gm_ref, dtf_ref, dt_ref, e_ref, f_ref, ed_ref, la_ref, cat_ref, kept_ref,
):
    row = lax.broadcasted_iota(jnp.int32, (CHUNK, CHUNK), 0)
    col = lax.broadcasted_iota(jnp.int32, (CHUNK, CHUNK), 1)
    lower = jnp.where(col <= row, 1.0, 0.0).astype(F32)
    used = col < 32
    heads = cat_ref.shape[1]
    before = jnp.zeros((1, CHUNK), F32)
    cw = cw_ref[...]
    for c in range(sh_ref.shape[0]):
        rows = rows_of(c)
        taps = conv_inputs(bc_ref[window_of(c)], sh_ref[c])
        k = conv_sum(taps, cw)
        act = k * sigmoid(k)
        b_act, c_act = act[:, :128], act[:, 128:]
        b_high, b_low = split2(b_act)
        c_high, c_low = split2(c_act)
        gram = mm_cols(c_high, b_high) + mm_cols(c_high, b_low) + mm_cols(c_low, b_high)
        gm_ref[rows] = gram * mask_ref[rows]
        b_ref[rows] = jnp.concatenate([b_high, b_low], axis=1)
        c_ref[rows] = jnp.concatenate([c_high, c_low], axis=1)
        bt_ref[:, rows] = jnp.concatenate(split2(b_act.T), axis=0)
        ct_ref[:, rows] = jnp.concatenate(split2(c_act.T), axis=0)
        step_in = dtr_ref[c * CHUNK + HALO : (c + 1) * CHUNK + HALO].astype(F32) + hp_ref[0:1]
        dt = jnp.where(used, softplus(step_in), 0.0)
        cumul = jnp.dot(lower, dt * hp_ref[1:2], precision=FULL, preferred_element_type=F32)
        last = cumul[CHUNK - 1 : CHUNK]
        cols = cols_ref[rows]
        e = jnp.where(used, jnp.exp2(cumul) * cols[:, 0:1], 0.0)
        f = jnp.where(used, jnp.exp2(last - cumul) * cols[:, 1:2], 0.0)
        ed = jnp.where(used, jnp.exp2(before + cumul) * cols[:, 2:3], 0.0)
        before = before + last
        dtf_ref[rows] = dt
        dt_ref[rows] = pack3(dt)
        e_ref[rows] = pack3(e)
        f_ref[rows] = pack3(f)
        ed_ref[rows] = pack3(ed)
        la_ref[rows] = pack3(cumul)
        cat_ref[c] = cumul.T[:heads]
        kept_ref[...] = jnp.broadcast_to(ed[CHUNK - 1 : CHUNK], kept_ref.shape)


def weights_of(c, step, la_ref, sel, cat_ref):
    spread = mm(la_ref[rows_of(c)], sel)
    per_step = LANES // HEAD
    out = []
    for i in range(per_step):
        ahead = cat_ref[c, pl.ds(step * per_step + i, 1), :]
        out.append(jnp.exp2(jnp.minimum(spread[:, i * CHUNK : (i + 1) * CHUNK] - ahead, 0.0)))
    return out


def head_pairs(x):
    first = lax.broadcasted_iota(jnp.int32, x.shape, 1) < HEAD
    zero = jnp.zeros_like(x)
    return jnp.concatenate([jnp.where(first, x, zero), jnp.where(first, zero, x)], axis=0)


def fwd_kernel(
    x_ref, sh_ref, cw_ref, gm_ref, c_ref, bt_ref, dt_ref, e_ref, f_ref, la_ref, sel_ref, exp_ref, cat_ref,
    y_ref, s_ref,
):
    step = pl.program_id(0)
    cw, sel, expand = cw_ref[...], sel_ref[...], exp_ref[...]
    state = jnp.zeros((128, LANES), F32)
    for c in range(sh_ref.shape[0]):
        rows = rows_of(c)
        k = conv_sum(conv_inputs(x_ref[window_of(c)], sh_ref[c]), cw)
        xa = k * sigmoid(k)
        v = mm(dt_ref[rows], expand) * xa
        ex = mm(e_ref[rows], expand)
        fx = mm(f_ref[rows], expand)
        v_parts = split2(v)
        gm = gm_ref[rows]
        weights = [w * gm for w in weights_of(c, step, la_ref, sel, cat_ref)]
        local = []
        for p in range(LANES // 128):
            own = tuple(head_pairs(part[:, p * 128 : (p + 1) * 128]) for part in v_parts)
            local.append(mm3(jnp.concatenate(weights[2 * p : 2 * p + 2], axis=1), own))
        y = jnp.concatenate(local, axis=1) + ex * mm3(pair_cols(c_ref[rows]), state)
        y_ref[rows] = y + cw[5:6] * xa
        state = ex[CHUNK - 1 : CHUNK] * state + mm3(pair_rows(bt_ref[:, rows]), fx * v)
    s_ref[...] = state.astype(BF16)


def gate_kernel(
    y_ref, z_ref, c_ref, ct_ref, ed_ref, sin_ref, wo_ref, exp_ref, expt_ref, gain_ref, hid_ref, df_ref,
    out_ref, fin_ref, dz_ref, dy_ref, q_ref, og_ref, gs_ref, acc_ref,
):
    i = pl.program_id(0)

    @pl.when(i == 0)
    def _():
        og_ref[...] = jnp.zeros_like(og_ref)
        acc_ref[...] = jnp.zeros_like(acc_ref)

    gain = gain_ref[0:1]
    inner = y_ref.shape[1]
    edx = mm(ed_ref[...], exp_ref[...])
    y_full = y_ref[...] + edx * (mm(c_ref[:, :128], sin_ref[...]) + mm(c_ref[:, 128:], sin_ref[...]))
    y = y_full.astype(BF16).astype(F32)
    z = z_ref[...].astype(F32)
    sig = sigmoid(z)
    sz = z * sig
    gated = y * sz
    gnorm = lax.rsqrt(jnp.sum(gated * gated, axis=1, keepdims=True) * (1.0 / inner) + EPS)
    normal = gated * gnorm
    final = (normal * gain).astype(BF16)
    fin_ref[...] = final
    out_ref[...] = (hid_ref[...].astype(F32) + mm(final, wo_ref[...])).astype(BF16)
    dfinal = df_ref[...]
    share = dfinal * normal
    og_ref[...] += jnp.sum(share.reshape(-1, 8, inner), axis=0)
    e = dfinal * gain
    mean = jnp.sum(share * gain, axis=1, keepdims=True) * (1.0 / inner)
    dgated = gnorm * (e - normal * mean)
    dz_ref[...] = (dgated * y * (sig * (1.0 + z * (1.0 - sig)))).astype(BF16)
    dyb = (dgated * sz).astype(BF16)
    dy_ref[...] = dyb
    dy = dyb.astype(F32)
    q_ref[...] = mm_split(dy * y_full, expt_ref[...])
    acc_ref[...] += mm3(pair_rows(ct_ref[...]), edx * dy)

    @pl.when(i == pl.num_programs(0) - 1)
    def _():
        gs_ref[...] = acc_ref[...].astype(BF16)


def back_kernel(
    x_ref, dy_ref, sh_ref, sht_ref, cw_ref, gm_ref, b_ref, bt_ref, ct_ref, dt_ref, e_ref, f_ref, la_ref,
    sel_ref, exp_ref, expt_ref, cat_ref, sin_ref, din_ref,
    dx_ref, edge_ref, cg_ref, m_ref, dcb_ref, red_ref, sd_ref,
    k_ref, states_ref, dxw_ref,
):
    step = pl.program_id(0)

    @pl.when(step == 0)
    def _():
        m_ref[...] = jnp.zeros_like(m_ref)
        dcb_ref[...] = jnp.zeros_like(dcb_ref)
        red_ref[...] = jnp.zeros_like(red_ref)

    count = sh_ref.shape[0]
    cw, sel, expand = cw_ref[...], sel_ref[...], exp_ref[...]
    state = sin_ref[...].astype(F32)
    for c in range(count):
        rows = rows_of(c)
        k = conv_sum(conv_inputs(x_ref[window_of(c)], sh_ref[c]), cw)
        k_ref[rows] = k
        v = mm(dt_ref[rows], expand) * (k * sigmoid(k))
        ex_last = mm(e_ref[rows], expand)[CHUNK - 1 : CHUNK]
        fx = mm(f_ref[rows], expand)
        states_ref[c] = state
        state = ex_last * state + mm3(pair_rows(bt_ref[:, rows]), fx * v)
    grad = din_ref[...].astype(F32)
    cg = [jnp.zeros((8, LANES), F32) for _ in range(TAPS + 1)]
    sd_ref[...] = jnp.zeros_like(sd_ref)
    after = state
    for c in reversed(range(count)):
        rows = rows_of(c)
        gradb = grad.astype(BF16)
        sd_ref[c : c + 1] = jnp.sum(after * grad, axis=0, keepdims=True)
        after = states_ref[c]
        taps = conv_inputs(x_ref[window_of(c)], sh_ref[c])
        k = k_ref[rows]
        sig = sigmoid(k)
        xa = k * sig
        dtx = mm(dt_ref[rows], expand)
        ex = mm(e_ref[rows], expand)
        fx = mm(f_ref[rows], expand)
        v = dtx * xa
        vb = v.astype(BF16)
        dyb = dy_ref[rows]
        dy = dyb.astype(F32)
        gm = gm_ref[rows]
        weights = weights_of(c, step, la_ref, sel, cat_ref)
        dv = []
        total = None
        for p in range(LANES // 128):
            lanes = slice(p * 128, (p + 1) * 128)
            pair = weights[2 * p : 2 * p + 2]
            products = mm_cols(dyb[:, lanes], head_pairs(vb[:, lanes]))
            part = products[:, :CHUNK] * pair[0] + products[:, CHUNK:] * pair[1]
            total = part if total is None else total + part
            stacked = jnp.concatenate([w * gm for w in pair], axis=0)
            own = head_pairs(dyb[:, lanes])
            high, low = split2(stacked)
            dv.append(mm_rows(high, own) + mm_rows(low, own))
        m_ref[rows] += total
        dv = jnp.concatenate(dv, axis=1) + fx * mm3(pair_cols(b_ref[rows]), grad)
        edy = ex * dy
        edyb = edy.astype(BF16)
        dcb_ref[rows, 0:128] += mm_cols((fx * v).astype(BF16), gradb)
        dcb_ref[rows, 128:256] += mm_cols(edyb, after.astype(BF16))
        grad = ex[CHUNK - 1 : CHUNK] * grad + mm3(pair_rows(ct_ref[:, rows]), edy)
        red = mm_split(xa * dv, expt_ref[:, 0:128])
        red += mm_split(v * dv, expt_ref[:, 128:256])
        red += mm_split(dy * xa, expt_ref[:, 256:384])
        red_ref[rows] += red
        dxa = dtx * dv + cw[5:6] * dy
        dk = dxa * (sig * (1.0 + k * (1.0 - sig)))
        cg[TAPS] += jnp.sum(dk.reshape(-1, 8, LANES), axis=0)
        for j in range(TAPS):
            cg[j] += jnp.sum((dk * taps[j]).reshape(-1, 8, LANES), axis=0)
        shifted = jnp.concatenate([(cw[j : j + 1] * dk).astype(BF16) for j in range(1, TAPS)], axis=0)
        moved = mm(sht_ref[c], shifted)
        low, high = c * CHUNK, (c + 1) * CHUNK
        own = cw[0:1] * dk
        dxw_ref[low : low + HALO] = moved[:HALO]
        dxw_ref[low + HALO : high] = moved[HALO:CHUNK] + own[: CHUNK - HALO]
        end = moved[CHUNK:] + own[CHUNK - HALO :]
        if c == count - 1:
            dxw_ref[high : high + HALO] = end
        else:
            dxw_ref[high : high + HALO] += end
    cg_ref[...] = jnp.zeros_like(cg_ref)
    for j in range(TAPS + 1):
        cg_ref[j : j + 1] = jnp.sum(cg[j], axis=0, keepdims=True)
    dx_ref[...] = dxw_ref[HALO:].astype(BF16)
    edge_ref[:HALO] = dxw_ref[:HALO]
    edge_ref[HALO:] = dxw_ref[count * CHUNK :]


def post_kernel(
    bc_ref, dtr_ref, sh_ref, sht_ref, mask_ref, cw_ref, hp_ref, b_ref, c_ref, m_ref, dcb_ref, red_ref, sd_ref,
    expt_ref, q_ref, dtf_ref,
    dbc_ref, ddt_ref, edge_ref, cg_ref, hg_ref,
    dxw_ref,
):
    count = sh_ref.shape[0]
    cw = cw_ref[...]
    width = bc_ref.shape[1]
    row = lax.broadcasted_iota(jnp.int32, (CHUNK, CHUNK), 0)
    col = lax.broadcasted_iota(jnp.int32, (CHUNK, CHUNK), 1)
    upper = jnp.where(col >= row, 1.0, 0.0).astype(F32)
    used = col < 32
    cg = [jnp.zeros((8, width), F32) for _ in range(TAPS + 1)]
    step_grad = jnp.zeros((8, CHUNK), F32)
    decay_grad = jnp.zeros((8, CHUNK), F32)
    skip_grad = jnp.zeros((8, CHUNK), F32)
    ends = mm_split(sd_ref[...], expt_ref[...])
    rate = hp_ref[2:3]
    for c in reversed(range(count)):
        rows = rows_of(c)
        taps = conv_inputs(bc_ref[window_of(c)], sh_ref[c])
        k = conv_sum(taps, cw)
        sig = sigmoid(k)
        both = (m_ref[rows] * mask_ref[rows]).astype(BF16)
        db = mm_rows(both, c_ref[rows, :128]) + dcb_ref[rows, 0:128]
        dc = mm(both, b_ref[rows, :128]) + dcb_ref[rows, 128:256]
        dk = jnp.concatenate([db, dc], axis=1) * (sig * (1.0 + k * (1.0 - sig)))
        cg[TAPS] += jnp.sum(dk.reshape(-1, 8, width), axis=0)
        for j in range(TAPS):
            cg[j] += jnp.sum((dk * taps[j]).reshape(-1, 8, width), axis=0)
        shifted = jnp.concatenate([(cw[j : j + 1] * dk).astype(BF16) for j in range(1, TAPS)], axis=0)
        moved = mm(sht_ref[c], shifted)
        low, high = c * CHUNK, (c + 1) * CHUNK
        own = cw[0:1] * dk
        dxw_ref[low : low + HALO] = moved[:HALO]
        dxw_ref[low + HALO : high] = moved[HALO:CHUNK] + own[: CHUNK - HALO]
        end = moved[CHUNK:] + own[CHUNK - HALO :]
        if c == count - 1:
            dxw_ref[high : high + HALO] = end
        else:
            dxw_ref[high : high + HALO] += end
        red = red_ref[rows]
        xdv = red
        vdv = pltpu.roll(red, 96, 1)
        dyx = pltpu.roll(red, 64, 1)
        change = q_ref[rows] - hp_ref[3:4] * dyx - vdv
        change = jnp.where(used, change, 0.0)
        da = jnp.dot(upper, change, precision=FULL, preferred_element_type=F32) + ends[c : c + 1]
        dt = dtf_ref[rows]
        step_in = dtr_ref[c * CHUNK + HALO : (c + 1) * CHUNK + HALO].astype(F32) + hp_ref[0:1]
        ddt = jnp.where(used, (xdv + rate * da) * sigmoid(step_in), 0.0)
        ddt_ref[rows] = ddt.astype(BF16)
        step_grad += jnp.sum(ddt.reshape(-1, 8, CHUNK), axis=0)
        decay_grad += jnp.sum((dt * da).reshape(-1, 8, CHUNK), axis=0)
        skip_grad += jnp.sum(dyx.reshape(-1, 8, CHUNK), axis=0)
    cg_ref[...] = jnp.zeros_like(cg_ref)
    for j in range(TAPS + 1):
        cg_ref[j : j + 1] = jnp.sum(cg[j], axis=0, keepdims=True)
    dbc_ref[...] = dxw_ref[HALO:].astype(BF16)
    edge_ref[:HALO] = dxw_ref[:HALO]
    edge_ref[HALO:] = dxw_ref[count * CHUNK :]
    hg_ref[...] = jnp.zeros_like(hg_ref)
    hg_ref[0:1] = jnp.sum(step_grad, axis=0, keepdims=True)
    hg_ref[1:2] = rate * jnp.sum(decay_grad, axis=0, keepdims=True)
    hg_ref[2:3] = jnp.sum(skip_grad, axis=0, keepdims=True)


def whole(array):
    return pl.BlockSpec(array.shape, lambda *_: (0,) * array.ndim)


def lanes_block(array, width=LANES, first=0):
    return pl.BlockSpec((array.shape[0], width), lambda i: (0, first + i))


def shape(dims, dtype=F32):
    return jax.ShapeDtypeStruct(dims, dtype)


PARAMS = pltpu.CompilerParams(vmem_limit_bytes=56 * 1024 * 1024, dimension_semantics=("arbitrary",))


def gather_rows(part):
    count = lax.axis_size(SEQ)
    share = part.shape[0] // count
    mine = lax.dynamic_slice_in_dim(part, lax.axis_index(SEQ) * share, share, 0)
    return lax.all_gather(mine, (WT, SEQ), axis=0, tiled=True)


def reduce_rows(part):
    count = lax.axis_size(SEQ)
    part = part.reshape(lax.axis_size(WT), count, -1, part.shape[1]).transpose(1, 0, 2, 3).reshape(part.shape)
    mine = lax.psum_scatter(part, SEQ, scatter_dimension=0, tiled=True)
    mine = lax.psum_scatter(mine, WT, scatter_dimension=0, tiled=True)
    return lax.all_gather(mine, SEQ, axis=0, tiled=True)


def shift_seq(x, by):
    count = lax.axis_size(SEQ)
    pairs = [(i, i + by) for i in range(count) if 0 <= i + by < count]
    return lax.ppermute(x, SEQ, pairs)


def carried(part, kept, hops, sign):
    total, fade = None, None
    for hop in range(1, hops + 1):
        moved = shift_seq(part, sign * hop).astype(F32)
        if fade is not None:
            moved = moved * fade
        total = moved if total is None else total + moved
        if hop < hops:
            factor = jnp.repeat(shift_seq(kept, sign * hop), HEAD)[None, :]
            fade = factor if fade is None else fade * factor
    return total.astype(BF16)


def on_device(
    hidden, doc_ids, norm_gain, in_weight, conv_weight, conv_bias, step_bias, decay_log, skip_gain, out_gain,
    out_weight, cotangent,
):
    seq_count = lax.axis_size(SEQ)
    seq_index = lax.axis_index(SEQ)
    inner = out_gain.shape[0]
    heads = step_bias.shape[0]
    length = hidden.shape[1]
    state_dim = (conv_weight.shape[1] - inner) // 2
    width = hidden.shape[2]
    chunks = length // CHUNK
    x_cols = in_weight.shape[1] - inner
    x_pad = -x_cols % 128
    bc_block = inner // (2 * state_dim)
    dt_block = (inner + 2 * state_dim) // 128
    hops = (doc_ids.shape[1] // 4 - 2) // length + 1
    hops = min(hops, seq_count - 1)

    w_x = gather_rows(jnp.pad(in_weight[:, inner:].astype(BF16), ((0, 0), (0, x_pad))))
    w_z = gather_rows(in_weight[:, :inner].astype(BF16))
    w_out = gather_rows(out_weight.astype(BF16))

    docs_all = jnp.concatenate([jnp.full((HALO,), -1, jnp.int32), doc_ids[0]])
    docs_ext = lax.dynamic_slice_in_dim(docs_all, seq_index * length, length + HALO, 0)
    docs = docs_ext[HALO:].reshape(chunks, CHUNK)
    windows = jnp.stack([docs_ext[c * CHUNK : (c + 1) * CHUNK + HALO] for c in range(chunks)])
    at_t = jnp.arange(CHUNK)
    at_s = jnp.arange(CHUNK + HALO)
    back = jnp.arange(1, TAPS)
    hits = (at_s[None, None, :] == at_t[None, :, None] + HALO - back[:, None, None])[None] & (
        windows[:, None, None, :] == docs[:, None, :, None]
    )
    shifts = hits.astype(BF16).reshape(chunks, (TAPS - 1) * CHUNK, CHUNK + HALO)
    hits_t = (at_s[:, None, None] == at_t[None, None, :] + HALO - back[None, :, None])[None] & (
        windows[:, :, None, None] == docs[:, None, None, :]
    )
    shifts_t = hits_t.astype(BF16).reshape(chunks, CHUNK + HALO, (TAPS - 1) * CHUNK)
    mask = ((docs[:, :, None] == docs[:, None, :]) & (at_t[None, :] <= at_t[:, None])[None]).astype(F32)
    mask = mask.reshape(length, CHUNK)
    enters = docs == windows[:, HALO - 1 : HALO]
    leaves = docs == docs[:, CHUNK - 1 :]
    enters_device = docs == docs_ext[HALO - 1]
    cols = jnp.stack([enters, leaves, enters_device], axis=-1).reshape(length, 3).astype(F32)
    cols = jnp.pad(cols, ((0, 0), (0, 125)))

    part = jnp.arange(128)[:, None]
    in_use = part < 3 * heads
    expand = ((part % heads == jnp.arange(inner)[None, :] // HEAD) & in_use).astype(BF16)
    select = ((part % heads == jnp.arange(heads * CHUNK)[None, :] // CHUNK) & in_use).astype(BF16)
    owner = jnp.arange(inner)[:, None] // HEAD
    lane = jnp.arange(384)[None, :]
    collect = (owner + (lane // 128) * heads == lane % 128).astype(BF16)

    rate = -jnp.exp(decay_log)
    head_rows = jnp.pad(jnp.stack([step_bias, rate * LOG2E, rate, skip_gain]), ((0, 4), (0, 128 - heads)))
    skip_row = jnp.pad(jnp.repeat(skip_gain, HEAD), (0, 2 * state_dim))
    conv_rows = jnp.concatenate([conv_weight, conv_bias[None], skip_row[None]], axis=0)
    conv_rows = jnp.pad(conv_rows, ((0, 2), (0, 0)))
    gain_rows = jnp.broadcast_to(out_gain[None], (8, inner))

    tail = lax.ppermute(hidden[0, length - HALO :], SEQ, [(i, i + 1) for i in range(seq_count - 1)])
    tokens = jnp.concatenate([tail, hidden[0]], axis=0).astype(F32)
    ratio_ext = lax.rsqrt(jnp.mean(tokens * tokens, axis=-1, keepdims=True) + EPS)
    normed_ext = (tokens * ratio_ext * norm_gain[None, :]).astype(BF16)
    tokens, ratio, normed = tokens[HALO:], ratio_ext[HALO:], normed_ext[HALO:]
    proj_x = mm(normed_ext, w_x).astype(BF16)
    gate = mm(normed, w_z).astype(BF16)
    grad_final = mm_cols(cotangent[0], w_out)

    bc_spec = pl.BlockSpec((length + HALO, 2 * state_dim), lambda i: (0, bc_block))
    dt_spec = pl.BlockSpec((length + HALO, 128), lambda i: (0, dt_block))
    bc_rows = conv_rows[:, inner:]
    outs = [
        shape((length, 256), BF16), shape((length, 256), BF16), shape((256, length), BF16), shape((256, length), BF16),
        shape((length, 128)), shape((length, 128)), shape((length, 128), BF16), shape((length, 128), BF16),
        shape((length, 128), BF16), shape((length, 128), BF16), shape((length, 128), BF16),
        shape((chunks, heads, CHUNK)), shape((8, 128)),
    ]
    ins = [shifts, mask, cols, bc_rows, head_rows]
    b_act, c_act, b_t, c_t, gram, dt_full, dt, e, f, ed, la, cat, kept = pl.pallas_call(
        prep_kernel,
        grid=(1,),
        in_specs=[bc_spec, dt_spec] + [whole(a) for a in ins],
        out_specs=[whole(o) for o in outs],
        out_shape=outs,
        compiler_params=PARAMS,
        name="prep",
    )(proj_x, proj_x, *ins)
    kept_row = kept[0, :heads]

    steps = inner // LANES
    sel_width = (LANES // HEAD) * CHUNK
    x_rows = conv_rows[:, :inner]
    y_local, state_part = pl.pallas_call(
        fwd_kernel,
        grid=(steps,),
        in_specs=[
            lanes_block(proj_x), whole(shifts), lanes_block(x_rows), whole(gram), whole(c_act), whole(b_t),
            whole(dt), whole(e), whole(f), whole(la), lanes_block(select, sel_width), lanes_block(expand), whole(cat),
        ],
        out_specs=[pl.BlockSpec((length, LANES), lambda i: (0, i)), pl.BlockSpec((128, LANES), lambda i: (0, i))],
        out_shape=[shape((length, inner)), shape((128, inner), BF16)],
        compiler_params=PARAMS,
        name="scan_fwd",
    )(proj_x, shifts, x_rows, gram, c_act, b_t, dt, e, f, la, select, expand, cat)
    state_in = carried(state_part, kept_row, hops, 1)

    def rows_spec(cols_):
        return pl.BlockSpec((CHUNK, cols_), lambda i: (i, 0))

    output, final, grad_gate, grad_mixed, q, gain_part, grad_state = pl.pallas_call(
        gate_kernel,
        grid=(chunks,),
        in_specs=[
            rows_spec(inner), rows_spec(inner), rows_spec(256), pl.BlockSpec((256, CHUNK), lambda i: (0, i)),
            rows_spec(128), whole(state_in), whole(w_out), whole(expand),
            pl.BlockSpec((inner, 128), lambda i: (0, 0)), whole(gain_rows), rows_spec(width), rows_spec(inner),
        ],
        out_specs=[
            rows_spec(width), rows_spec(inner), rows_spec(inner), rows_spec(inner), rows_spec(128),
            pl.BlockSpec((8, inner), lambda i: (0, 0)), pl.BlockSpec((128, inner), lambda i: (0, 0)),
        ],
        out_shape=[
            shape((length, width), BF16), shape((length, inner), BF16), shape((length, inner), BF16),
            shape((length, inner), BF16), shape((length, 128)), shape((8, inner)), shape((128, inner), BF16),
        ],
        scratch_shapes=[pltpu.VMEM((128, inner), F32)],
        compiler_params=PARAMS,
        name="gate",
    )(y_local, gate, c_act, c_t, ed, state_in, w_out, expand, collect, gain_rows, hidden[0], grad_final)
    grad_in = carried(grad_state, kept_row, hops, -1)

    out_weight_part = mm_rows(final, cotangent[0])
    in_z_part = mm_rows(normed, grad_gate)
    grad_normed_z = mm_cols(grad_gate, w_z)

    block = lambda rows_: pl.BlockSpec((rows_, LANES), lambda i: (0, i))
    acc = lambda rows_, cols_: pl.BlockSpec((rows_, cols_), lambda i: (0, 0))
    grad_x, edge_x, cg_x, pair_sum, dcb, red, ends = pl.pallas_call(
        back_kernel,
        grid=(steps,),
        in_specs=[
            lanes_block(proj_x), lanes_block(grad_mixed), whole(shifts), whole(shifts_t), lanes_block(x_rows),
            whole(gram), whole(b_act), whole(b_t), whole(c_t), whole(dt), whole(e), whole(f), whole(la),
            lanes_block(select, sel_width), lanes_block(expand), pl.BlockSpec((LANES, 384), lambda i: (i, 0)),
            whole(cat), lanes_block(state_in), lanes_block(grad_in),
        ],
        out_specs=[
            block(length), block(2 * HALO), block(8), acc(length, 128), acc(length, 256), acc(length, 128), block(8),
        ],
        out_shape=[
            shape((length, inner), BF16), shape((2 * HALO, inner)), shape((8, inner)), shape((length, 128)),
            shape((length, 256)), shape((length, 128)), shape((8, inner)),
        ],
        scratch_shapes=[
            pltpu.VMEM((length, LANES), F32), pltpu.VMEM((chunks, 128, LANES), F32),
            pltpu.VMEM((length + HALO, LANES), F32),
        ],
        compiler_params=PARAMS,
        name="scan_bwd",
    )(proj_x, grad_mixed, shifts, shifts_t, x_rows, gram, b_act, b_t, c_t, dt, e, f, la, select, expand, collect,
      cat, state_in, grad_in)

    ins = [shifts, shifts_t, mask, bc_rows, head_rows, b_act, c_act, pair_sum, dcb, red, ends, collect, q, dt_full]
    in_specs = [whole(a) for a in ins]
    in_specs[11] = acc(inner, 128)
    outs = [
        shape((length, 2 * state_dim), BF16), shape((length, 128), BF16), shape((2 * HALO, 2 * state_dim)),
        shape((8, 2 * state_dim)), shape((8, 128)),
    ]
    grad_bc, grad_dt, edge_bc, cg_bc, head_grads = pl.pallas_call(
        post_kernel,
        grid=(1,),
        in_specs=[bc_spec, dt_spec] + in_specs,
        out_specs=[whole(o) for o in outs],
        out_shape=outs,
        scratch_shapes=[pltpu.VMEM((length + HALO, 2 * state_dim), F32)],
        compiler_params=PARAMS,
        name="post",
    )(proj_x, proj_x, *ins)

    edge = jnp.concatenate([edge_x, edge_bc], axis=1)
    from_next = shift_seq(edge[:HALO], -1)
    last_rows = (edge[HALO:] + from_next).astype(BF16)
    grad_conv = jnp.concatenate([grad_x, grad_bc], axis=1)
    grad_conv = jnp.concatenate([grad_conv[: length - HALO], last_rows], axis=0)
    grad_proj_x = jnp.concatenate([grad_conv, grad_dt], axis=1)

    in_x_part = mm_rows(normed, grad_proj_x)
    grad_normed = grad_normed_z + mm_cols(grad_proj_x, w_x)
    norm_gain_part = jnp.sum(grad_normed * tokens * ratio, axis=0)
    scaled_in = grad_normed * norm_gain[None, :]
    input_grad = (
        cotangent[0].astype(F32)
        + ratio * scaled_in
        - tokens * ratio * ratio * ratio * jnp.mean(scaled_in * tokens, axis=-1, keepdims=True)
    )

    small = jnp.concatenate(
        [
            norm_gain_part,
            jnp.sum(gain_part, axis=0),
            jnp.concatenate([cg_x, cg_bc], axis=1)[: TAPS + 1].reshape(-1),
            head_grads[:3, :heads].reshape(-1),
        ]
    )
    small = lax.psum(small, (SEQ, WT))
    at = 0
    pieces = []
    for size in (width, inner, TAPS * conv_bias.shape[0], conv_bias.shape[0], heads, heads, heads):
        pieces.append(small[at : at + size])
        at += size
    norm_total, gain_total, conv_w_total, conv_b_total, step_total, decay_total, skip_total = pieces

    out_grad = reduce_rows(out_weight_part).astype(F32)
    in_z = reduce_rows(in_z_part)
    in_x = reduce_rows(in_x_part)
    in_grad = jnp.concatenate([in_z, in_x[:, :x_cols]], axis=1).astype(F32)
    return (
        output[None], input_grad[None], norm_total, in_grad, conv_w_total.reshape(conv_weight.shape), conv_b_total,
        step_total, decay_total, skip_total, gain_total, out_grad,
    )


def solution(mesh):
    placed = (
        P(WT, SEQ, None), P(WT, None), P(), P(WT, None), P(), P(), P(), P(), P(), P(), P(WT, None), P(WT, SEQ, None),
    )
    return jax.shard_map(
        on_device,
        mesh=mesh,
        in_specs=placed,
        out_specs=(
            P(WT, SEQ, None), P(WT, SEQ, None), P(), P(WT, None), P(), P(), P(), P(), P(), P(), P(WT, None),
        ),
        check_vma=False,
    )
```

time: 1990 us -> 689 us (0.35)
  local copies, waits for them, and re-layouts: 434 us -> 48.7 us
  matrix products: 358 us -> 43.5 us
  waiting for transfers between devices: 709 us -> 406 us
  other arithmetic: 320 us -> 23.2 us
  Pallas kernels: 0 us -> 87.3 us
  loops' own time: 46.6 us -> 0 us
  blocking collectives: 72.4 us -> 40 us
    dot_general x230 -> x8, matrix products: 358 us -> 43.5 us  [the longest x3 20.7 us: mm_cols(): lax.dot_general(a, b, (((1,), (1,)), ((), ())), preferred_element_type=F32)]
    reduce_scatter x3 -> x6, waiting for transfers between devices: 424 us -> 214 us  [the longest x3 126 us: reduce_rows(): mine = lax.psum_scatter(part, SEQ, scatter_dimension=0, tiled=True)]
    dynamic_update_slice x51 -> x0, local copies, waits for them, and re-layouts: 152 us -> none  [the longest x48 151 us: ssd(): lax.scan(step_fn, start_carry, (x_blocks, b_blocks, c_blocks, dt_blocks,...]
    another operation x146 -> x4, other arithmetic: 145 us -> 0.64 us  [the longest x2 0.61 us: on_device(): jnp.stack([step_bias, rate * LOG2E, rate, skip_gain])]
    pallas_call x0 -> x5, Pallas kernels: none -> 87.3 us  [the longest x1 40.8 us: on_device(): pl.pallas_call(back_kernel, grid=(steps,), in_specs=[lanes_block(proj_x),...]
    all_to_all x5 -> x0, waiting for transfers between devices: 77.8 us -> none  [the longest x1 29.3 us: on_device(): lax.all_to_all(grad_x.astype(jnp.bfloat16), 'seq', split_axis=0, concat_a...]
    dynamic_slice x66 -> x3, local copies, waits for them, and re-layouts: 72.4 us -> 3.24 us  [the longest x2 3.16 us: gather_rows(): mine = lax.dynamic_slice_in_dim(part, lax.axis_index(SEQ) * share, share, 0)]
    squeeze x80 -> x2, local copies, waits for them, and re-layouts: 59 us -> 0.69 us  [the longest x1 0.69 us: on_device(): kept_row = kept[0, :heads]]
  transfers between devices with their start and end apart: 12 -> 20, of which waited for: 8 -> 12; matrix products, arithmetic and copies ran while one was open for 18% -> 12% of each run, Pallas kernels for 0% -> 10%
where the time goes in v1:
time: 689 us; the launch traced here: 681 us
  waiting for transfers between devices  406 us (59%)
  Pallas kernels  87.3 us (13%)
  local copies, waits for them, and re-layouts  48.7 us (7%)
  matrix products  43.5 us (6%)
  blocking collectives  40 us (6%)
  other arithmetic  23.2 us (3%)
  starting transfers between devices  17.3 us (3%)
  between operations  15.2 us (2%)
    all_gather x3, waiting for transfers between devices, gather_rows(): return lax.all_gather(mine, (WT, SEQ), axis=0, tiled=True)  133 us
    reduce_scatter x3, waiting for transfers between devices, reduce_rows(): mine = lax.psum_scatter(part, SEQ, scatter_dimension=0, tiled=True)  126 us
    reduce_scatter x3, waiting for transfers between devices, reduce_rows(): mine = lax.psum_scatter(mine, WT, scatter_dimension=0, tiled=True)  88.4 us
    pallas_call x1, Pallas kernels, on_device(): pl.pallas_call(back_kernel, grid=(steps,), in_specs=[lanes_block(proj_x),...  40.8 us
    psum x1, blocking collectives, on_device(): small = lax.psum(small, (SEQ, WT))  40 us
    ppermute x7, waiting for transfers between devices, shift_seq(): return lax.ppermute(x, SEQ, pairs)  29.3 us
    all_gather x3, waiting for transfers between devices, reduce_rows(): return lax.all_gather(mine, SEQ, axis=0, tiled=True)  28.3 us
    dot_general x3, matrix products, mm_cols(): lax.dot_general(a, b, (((1,), (1,)), ((), ())), preferred_element_type=F32)  20.7 us
  transfers between devices with their start and end apart: 20, of which 12 were waited for; matrix products, arithmetic and copies ran while one was open for 12% of the time, Pallas kernels for 10%

profile of v1, /device:TPU:0, one launch (start us, length us, event | category | flops | bytes accessed | tf_op | source)
XLA Modules:
  0.0 681.0 jit_solution(823952903273360471)
XLA Ops:
  7.2 1.8 slice.128
  9.1 1.4 copy.61
  10.5 1.6 constant_dynamic-slice_fusion
  12.1 2.8 slice.123
  15.0 2.5 copy.60
  17.5 1.6 pad_dynamic-slice_fusion
  19.1 0.7 dynamic-slice_convert_fusion
  19.9 2.4 collective-permute-start
  23.3 0.7 bitcast_compare_fusion.2
  24.6 0.7 pad_convert_fusion.cols_ref
  25.7 1.0 and_convert_fusion.1.exp_ref
  26.8 1.5 fusion.5.expt_ref
  28.3 1.4 and_convert_fusion.sel_ref
  31.5 1.1 fusion.9.sh_ref
  32.6 0.9 fusion.18.mask_ref
  34.1 42.9 %all-gather.9.cloned.1.call-done = bf16[1024,2048]{1,0:T(8,128)(2,1)} async-done(((bf16[32,2048]{1,0:T(8,128)(2,1)}), bf16[1024,2048]{1,0:T(8,128)(2,1)}) %all-gather.9.cloned.1.call-update) | async-done | bytes 4194320 | tf_op jit(solution)/shard_map/all_gather | solution.py:412
  76.9 5.8 convolution_convert_fusion.1.z_ref
  82.8 60.8 %all-gather.7.cloned.1.call-done = bf16[1024,2432]{1,0:T(8,128)(2,1)} async-done(((bf16[32,2432]{1,0:T(8,128)(2,1)}), bf16[1024,2432]{1,0:T(8,128)(2,1)}) %all-gather.7.cloned.1.call-update) | async-done | bytes 4980752 | tf_op jit(solution)/shard_map/all_gather | solution.py:412
  143.6 6.6 convolution_convert_fusion.bc_ref.dtr_ref.x_ref
  150.2 4.0 prep.1
  154.3 19.6 %scan_fwd.1 = (f32[512,2048]{1,0:T(8,128)}, bf16[128,2048]{1,0:T(8,128)(2,1)}) custom-call(bf16[528,2432]{1,0:T(8,128)(2,1)} %convolution_convert_fusion.bc_ref.dtr_ref.x_ref, bf16[4,384,144]{2,1,0:T(8,128)(2,1)} %fusion.9.sh_ref, f32[8,2048]{1,0:T(8,128)} %slice.124.cw_ref, f32[512,128]{1,0:T(8,128)} %get-tuple-element.45.gm_ref, ...), custom_call_target="tpu_custom_call" | custom-call | tf_op jit(solution)/shard_map/scan_fwd/pallas_call | solution.py:536
  173.8 2.2 collective-permute-start.1
  176.0 3.2 collective-permute-start.2
  179.2 0.7 slice_bitcast_fusion.1
  179.9 3.4 collective-permute-start.3
  183.4 29.5 %all-gather.11.cloned.1.call-done.wo_ref = bf16[2048,1024]{1,0:T(8,128)(2,1)} async-done(((bf16[64,1024]{1,0:T(8,128)(2,1)}), bf16[2048,1024]{1,0:T(8,128)(2,1)}) %all-gather.11.cloned.1.call-update) | async-done | bytes 4194320 | tf_op jit(solution)/shard_map/all_gather | solution.py:412
  212.8 6.6 convolution_bitcast_fusion.df_ref
  219.6 1.0 add_convert_fusion.1.sin_ref
  221.2 17.2 %gate.1 = (bf16[512,1024]{1,0:T(8,128)(2,1)}, bf16[512,2048]{1,0:T(8,128)(2,1)}, bf16[512,2048]{1,0:T(8,128)(2,1)}, bf16[512,2048]{1,0:T(8,128)(2,1)}, f32[512,1...) custom-call(f32[512,2048]{1,0:T(8,128)} %get-tuple-element.53.y_ref, ...), custom_call_target="tpu_custom_call" | custom-call | tf_op jit(solution)/shard_map/gate/pallas_call | solution.py:553
  238.4 2.9 copy.55
  241.3 2.5 convolution_bitcast_fusion.1
  243.7 4.1 copy.56
  248.0 1.2 copy-done.5
  249.1 4.0 fusion.14
  253.1 5.2 copy.53
  258.4 1.3 collective-permute-start.4
  259.7 1.5 collective-permute-start.5
  262.1 1.3 collective-permute-start.6
  263.4 0.9 and_convert_fusion.2.sht_ref
  264.3 1.5 collective-permute-done.6
  265.9 25.9 %collective-permute-done.5 = bf16[128,2048]{1,0:T(8,128)(2,1)} collective-permute-done((bf16[128,2048]{1,0:T(8,128)(2,1)}, bf16[128,2048]{1,0:T(8,128)(2,1)}, u32[]{:S(2)}, u32[]{:S(2)}) %collective-permute-start.5) | collective-permute-done | bytes 524320 | tf_op jit(solution)/shard_map/ppermute | solution.py:426
  291.8 2.2 add_convert_fusion.din_ref
  294.0 40.8 %scan_bwd.1 = (bf16[512,2048]{1,0:T(8,128)(2,1)}, f32[32,2048]{1,0:T(8,128)}, f32[8,2048]{1,0:T(8,128)}, f32[512,128]{1,0:T(8,128)}, f32[512,256]{1,0:T(8,128)}, /*index=5*/f32[512,128]{1,0:T(8,128)}, f32[8,2048]{1,0:T(8,128)}) custom-call(bf16[528,2432]{1,0:T(8,128)(2,1)} %convolution_convert_fusion.bc_ref.dtr_ref.x_ref, ...), custom_call_target="tpu_custom_call" | custom-call | tf_op jit(solution)/shard_map/scan_bwd/pallas_call | solution.py:581
  334.8 5.8 post.1
  340.6 0.8 constant_dynamic-update-slice_fusion
  341.3 1.3 collective-permute-start.7
  342.6 2.0 collective-permute-done.7
  344.6 3.9 fusion.12
  348.6 4.8 copy.54
  353.5 0.7 reduce-scatter.17.cloned.1.call-update
  354.2 43.4 %reduce-scatter.7.cloned.1.call-done = f32[128,2048]{1,0:T(8,128)} async-done(((f32[1024,2048]{1,0:T(8,128)}), f32[128,2048]{1,0:T(8,128)}) %reduce-scatter.7.cloned.1.call-update) | async-done | bytes 1048592 | tf_op jit(solution)/shard_map/reduce_scatter | solution.py:418
  397.7 82.3 %reduce-scatter.11.cloned.1.call-done = f32[128,2432]{1,0:T(8,128)} async-done(((f32[1024,2432]{1,0:T(8,128)}), f32[128,2432]{1,0:T(8,128)}) %reduce-scatter.11.cloned.1.call-update) | async-done | bytes 1245200 | tf_op jit(solution)/shard_map/reduce_scatter | solution.py:418
  480.0 29.4 %reduce-scatter.17.cloned.1.call-done = f32[64,1024]{1,0:T(8,128)} async-done(((f32[256,1024]{1,0:T(8,128)}), f32[64,1024]{1,0:T(8,128)}) %reduce-scatter.17.cloned.1.call-update) | async-done | bytes 262160 | tf_op jit(solution)/shard_map/reduce_scatter | solution.py:419
  509.5 28.1 %reduce-scatter.9.cloned.1.call-done = f32[32,2048]{1,0:T(8,128)} async-done(((f32[128,2048]{1,0:T(8,128)}), f32[32,2048]{1,0:T(8,128)}) %reduce-scatter.9.cloned.1.call-update) | async-done | bytes 262160 | tf_op jit(solution)/shard_map/reduce_scatter | solution.py:419
  538.0 30.9 %reduce-scatter.13.cloned.1.call-done = f32[32,2432]{1,0:T(8,128)} async-done(((f32[128,2432]{1,0:T(8,128)}), f32[32,2432]{1,0:T(8,128)}) %reduce-scatter.13.cloned.1.call-update) | async-done | bytes 311312 | tf_op jit(solution)/shard_map/reduce_scatter | solution.py:419
  569.0 1.6 maximum_convert_fusion
  570.6 6.5 fusion.40
  577.3 7.5 %multiply_reduce_fusion.1 = (f32[1024]{0:T(1024)S(1)}, f32[512]{0:T(512)S(1)}, f32[512,1024]{1,0:T(8,128)S(1)}) fusion(f32[528,1024]{1,0:T(8,128)} %maximum_convert_fusion, f32[512]{0:T(512)S(1)} %slice.108, f32[1024]{0:T(1024)S(1)} %copy-done.11, f32[512,1024]{1,0:T(8,128)} %fusion.40, bf16[1024,2432]{1,0:T(8,128)(2,1)} %all-gather.7.cloned.1.call-done, ...), kind=kOutput, calls=%fused_computation.19 | convolution fusion | flops 2572483072 | bytes 13848576 | tf_op jit(solution)/shard_map/dot_general | solution.py:29
  584.9 40.0 %psum.7 = f32[14688]{0:T(1024)S(1)} all-reduce(f32[14688]{0:T(1024)S(1)} %pad_maximum_fusion.2), channel_id=1, replica_groups=mesh['seq'=8,'wt'=4] {'seq','wt'}, use_global_device_ids=true, to_apply=%region_4.5 | all-reduce | flops 14688 | bytes 117504 | tf_op jit(solution)/shard_map/psum | solution.py:649
  627.9 3.6 subtract_bitcast_fusion
  631.5 28.3 %all-gather.15.cloned.1.call-done = f32[256,2432]{1,0:T(8,128)} async-done(((f32[32,2432]{1,0:T(8,128)}), f32[256,2432]{1,0:T(8,128)}) %all-gather.15.cloned.1.call-update) | async-done | bytes 2490384 | tf_op jit(solution)/shard_map/all_gather | solution.py:420
  659.8 4.8 pad_maximum_fusion
  664.6 6.0 copy.57
  670.6 3.2 copy.64
  (136 shorter events, 10.3 us)
Async XLA Ops:
  7.2 12.0 %copy-start = (f32[512,1024]{1,0:T(8,128)S(1)}, f32[512,1024]{1,0:T(8,128)}, u32[]{:S(2)}) copy-start(f32[512,1024]{1,0:T(8,128)} %param.22) | copy-start | bytes 6291460
  7.2 69.7 %all-gather.9.cloned.1.call-start = ((), (), s32[]{:S(2)}) async-start(), calls=%async_computation.7 | async-start | bytes 4325376 | tf_op jit(solution)/shard_map/all_gather | solution.py:412
  12.1 131.5 %all-gather.7.cloned.1.call-start = ((), (), s32[]{:S(2)}) async-start(), calls=%async_computation.6 | async-start | bytes 5136384 | tf_op jit(solution)/shard_map/all_gather | solution.py:412
  15.0 5.0 copy-start.2
  15.0 7.3 %copy-start.12 = (s32[1,4096]{1,0:T(1,128)S(1)}, s32[1,4096]{1,0:T(1,128)}, u32[]{:S(2)}) copy-start(s32[1,4096]{1,0:T(1,128)} %param.13) | copy-start | bytes 49156
  15.0 9.3 %copy-start.16 = (f32[32]{0:T(128)S(1)}, f32[32]{0:T(128)}, u32[]{:S(2)}) copy-start(f32[32]{0:T(128)} %param.20) | copy-start | bytes 388
  15.0 9.5 %copy-start.13 = (f32[2304]{0:T(1024)S(1)}, f32[2304]{0:T(1024)}, u32[]{:S(2)}) copy-start(f32[2304]{0:T(1024)} %param.17) | copy-start | bytes 27652
  15.0 10.3 %copy-start.21 = (f32[32]{0:T(128)S(1)}, f32[32]{0:T(128)}, u32[]{:S(2)}) copy-start(f32[32]{0:T(128)} %param.19) | copy-start | bytes 388
  15.0 10.7 %copy-start.10 = (f32[4,2304]{1,0:T(4,128)S(1)}, f32[4,2304]{1,0:T(4,128)}, u32[]{:S(2)}) copy-start(f32[4,2304]{1,0:T(4,128)} %param.16) | copy-start | bytes 110596
  19.1 193.7 %all-gather.11.cloned.1.call-start = ((), (), s32[]{:S(2)}) async-start(), calls=%async_computation.8 | async-start | bytes 4325376 | tf_op jit(solution)/shard_map/all_gather | solution.py:412
  19.9 9.8 %copy-start.18 = (f32[32]{0:T(128)S(1)}, f32[32]{0:T(128)}, u32[]{:S(2)}) copy-start(f32[32]{0:T(128)} %param.18) | copy-start | bytes 388
  19.9 333.6 %reduce-scatter.15.cloned.1.call-start = ((), (), s32[]{:S(2)}) async-start(), calls=%async_computation.15 | async-start | bytes 9437184 | tf_op jit(solution)/shard_map/reduce_scatter | solution.py:418
  19.9 13.5 %collective-permute-start = (bf16[16,1024]{1,0:T(8,128)(2,1)S(1)}, bf16[16,1024]{1,0:T(8,128)(2,1)S(1)}, u32[]{:S(2)}, u32[]{:S(2)}) collective-permute-start(bf16[16,1024]{1,0:T(8,128)(2,1)S(1)} %slice_bitcast_fusion), channel_id=1, source_target_pairs={{0,4},{4,8},{8,12},{12,16},{16,20},{20,24},{24,28},{1,5},{5,9},{9,... | collective-permute-start | bytes 98312 | tf_op jit(solution)/shard_map/ppermute | solution.py:503
  28.3 5.4 copy-start.11
  34.0 109.6 %copy-start.4 = (bf16[528,1024]{1,0:T(8,128)(2,1)}, bf16[528,1024]{1,0:T(8,128)(2,1)S(1)}, u32[]{:S(2)}) copy-start(bf16[528,1024]{1,0:T(8,128)(2,1)S(1)} %multiply_convert_fusion) | copy-start | bytes 3244036
  154.3 58.6 %copy-start.6 = (bf16[1,512,1024]{2,1,0:T(8,128)(2,1)S(1)}, bf16[1,512,1024]{2,1,0:T(8,128)(2,1)}, u32[]{:S(2)}) copy-start(bf16[1,512,1024]{2,1,0:T(8,128)(2,1)} %param.23) | copy-start | bytes 3145732
  173.8 45.8 %collective-permute-start.1 = (bf16[128,2048]{1,0:T(8,128)(2,1)}, bf16[128,2048]{1,0:T(8,128)(2,1)S(1)}, u32[]{:S(2)}, u32[]{:S(2)}) collective-permute-start(bf16[128,2048]{1,0:T(8,128)(2,1)} %get-tuple-element.56), channel_id=1, source_target_pairs={{0,4},{4,8},{8,12},{12,16},{16,20},{20,24},{24,28},{1,5},{5,9},{9,... | collective-permute-start | bytes 1572872 | tf_op jit(solution)/shard_map/ppermute | solution.py:426
  176.0 43.5 %collective-permute-start.2 = (bf16[128,2048]{1,0:T(8,128)(2,1)}, bf16[128,2048]{1,0:T(8,128)(2,1)S(1)}, u32[]{:S(2)}, u32[]{:S(2)}) collective-permute-start(bf16[128,2048]{1,0:T(8,128)(2,1)} %get-tuple-element.56), channel_id=1, source_target_pairs={{0,8},{4,12},{8,16},{12,20},{16,24},{20,28},{1,9},{5,13},{9,17},{1... | collective-permute-start | bytes 1572872 | tf_op jit(solution)/shard_map/ppermute | solution.py:426
  179.9 40.6 %copy-start.14 = (f32[2048]{0:T(1024)S(1)}, f32[2048]{0:T(1024)}, u32[]{:S(2)}) copy-start(f32[2048]{0:T(1024)} %param.21) | copy-start | bytes 24580
  179.9 39.5 %collective-permute-start.3 = (f32[32]{0:T(128)S(1)}, f32[32]{0:T(128)S(1)}, u32[]{:S(2)}, u32[]{:S(2)}) collective-permute-start(f32[32]{0:T(128)S(1)} %slice_bitcast_fusion.1), channel_id=1, source_target_pairs={{0,4},{4,8},{8,12},{12,16},{16,20},{20,24},{24,28},{1,5},{5,9},{9,... | collective-permute-start | bytes 392 | tf_op jit(solution)/shard_map/ppermute | solution.py:426
  247.9 1.2 copy-start.5
  247.9 149.7 %reduce-scatter.7.cloned.1.call-start = ((), (), s32[]{:S(2)}) async-start(), calls=%async_computation.9 | async-start | bytes 9437184 | tf_op jit(solution)/shard_map/reduce_scatter | solution.py:418
  258.4 221.6 %reduce-scatter.11.cloned.1.call-start = ((), (), s32[]{:S(2)}) async-start(), calls=%async_computation.12 | async-start | bytes 11206656 | tf_op jit(solution)/shard_map/reduce_scatter | solution.py:418
  258.4 7.5 %collective-permute-start.4 = (bf16[128,2048]{1,0:T(8,128)(2,1)}, bf16[128,2048]{1,0:T(8,128)(2,1)}, u32[]{:S(2)}, u32[]{:S(2)}) collective-permute-start(bf16[128,2048]{1,0:T(8,128)(2,1)} %get-tuple-element.62), channel_id=1, source_target_pairs={{4,0},{8,4},{12,8},{16,12},{20,16},{24,20},{28,24},{5,1},{9,5},{13... | collective-permute-start | bytes 1572872 | tf_op jit(solution)/shard_map/ppermute | solution.py:426
  259.7 32.1 %collective-permute-start.5 = (bf16[128,2048]{1,0:T(8,128)(2,1)}, bf16[128,2048]{1,0:T(8,128)(2,1)}, u32[]{:S(2)}, u32[]{:S(2)}) collective-permute-start(bf16[128,2048]{1,0:T(8,128)(2,1)} %get-tuple-element.62), channel_id=1, source_target_pairs={{8,0},{12,4},{16,8},{20,12},{24,16},{28,20},{9,1},{13,5},{17,9},{2... | collective-permute-start | bytes 1572872 | tf_op jit(solution)/shard_map/ppermute | solution.py:426
  262.1 3.6 collective-permute-start.6
  334.7 5.8 copy-start.7
  334.7 9.9 %copy-start.19 = (bf16[512,2048]{1,0:T(8,128)(2,1)S(1)}, bf16[512,2048]{1,0:T(8,128)(2,1)}, u32[]{:S(2)}) copy-start(bf16[512,2048]{1,0:T(8,128)(2,1)} %get-tuple-element.63) | copy-start | bytes 6291460
  341.3 3.3 collective-permute-start.7
  353.4 215.5 %copy-start.3 = (bf16[1,512,1024]{2,1,0:T(8,128)(2,1)S(1)}, bf16[1,512,1024]{2,1,0:T(8,128)(2,1)}, u32[]{:S(2)}) copy-start(bf16[1,512,1024]{2,1,0:T(8,128)(2,1)} %param.12) | copy-start | bytes 3145732
  353.4 156.0 %reduce-scatter.17.cloned.1.call-start = ((), (), s32[]{:S(2)}) async-start(), calls=%async_computation.16 | async-start | bytes 1310720 | tf_op jit(solution)/shard_map/reduce_scatter | solution.py:419
  354.2 183.5 %reduce-scatter.9.cloned.1.call-start = ((), (), s32[]{:S(2)}) async-start(), calls=%async_computation.10 | async-start | bytes 1310720 | tf_op jit(solution)/shard_map/reduce_scatter | solution.py:419
  397.7 171.2 %reduce-scatter.13.cloned.1.call-start = ((), (), s32[]{:S(2)}) async-start(), calls=%async_computation.13 | async-start | bytes 1556480 | tf_op jit(solution)/shard_map/reduce_scatter | solution.py:419
  480.0 90.6 %copy-start.8 = (f32[8,2048]{1,0:T(8,128)S(1)}, f32[8,2048]{1,0:T(8,128)}, u32[]{:S(2)}) copy-start(f32[8,2048]{1,0:T(8,128)} %get-tuple-element.74) | copy-start | bytes 196612
  480.0 151.5 %all-gather.17.cloned.1.call-start = ((), (), s32[]{:S(2)}) async-start(), calls=%async_computation.17 | async-start | bytes 2359296 | tf_op jit(solution)/shard_map/all_gather | solution.py:420
  509.5 122.0 %all-gather.13.cloned.1.call-start = ((), (), s32[]{:S(2)}) async-start(), calls=%async_computation.11 | async-start | bytes 2359296 | tf_op jit(solution)/shard_map/all_gather | solution.py:420
  537.7 122.1 %all-gather.15.cloned.1.call-start = ((), (), s32[]{:S(2)}) async-start(), calls=%async_computation.14 | async-start | bytes 2801664 | tf_op jit(solution)/shard_map/all_gather | solution.py:420
  570.6 6.6 copy-start.9
  570.6 6.6 copy-start.15
  570.6 6.6 copy-start.17
  570.6 6.7 copy-start.20
  664.6 9.2 %copy-start.1 = (f32[512,1024]{1,0:T(8,128)S(1)}, f32[512,1024]{1,0:T(8,128)}, u32[]{:S(2)}) copy-start(f32[512,1024]{1,0:T(8,128)} %param.22) | copy-start | bytes 6291460
Sparse Core Ops, SparseCore 0:
  12.2 64.6 all-gather.8
  80.3 63.2 all-gather.6
  146.5 66.2 all-gather.10
  248.0 74.5 reduce-scatter.14
  326.3 71.2 reduce-scatter.6
  401.1 78.8 reduce-scatter.10
  482.3 27.1 reduce-scatter.16
  511.8 25.7 reduce-scatter.8
  540.0 28.8 reduce-scatter.12
  570.8 27.1 all-gather.16
  600.0 28.3 all-gather.12
  630.3 29.4 all-gather.14
